TPU v7x, 128 devices: a whole 4x4x4 slice. The times are simulated.
128 devices in a mesh: rows: 32 (over y, z, core), cols: 4 (over x).
Axes of the slice: x: 4, y: 4, z: 4, core: 2. Of those that a mesh axis runs over, the one named last changes fastest.
Arguments:
- points: float32 [16, 1048576], P(None, ('rows', 'cols')), may hold values from -2 to 2
- coeffs: float32 [32, 1048576], P(None, ('rows', 'cols')), may hold values from -6 to 6
- velocity: float32 [32, 1048576], P(None, ('rows', 'cols')), may hold values from -4 to 4
- targets: float32 [32, 1048576], P(None, ('rows', 'cols')), may hold values from -6 to 6
- batch_index: int32 [2, 2048], replicated, may hold values from 0 to 1048575, as said below
- test_points: float32 [16, 4096], P(None, 'cols'), may hold values from -2 to 2
Outputs:
- coeffs_out: float32 [32, 1048576], P(None, ('rows', 'cols'))
- velocity_out: float32 [32, 1048576], P(None, ('rows', 'cols'))
- samples: float32 [32, 4096], P(None, 'cols')
Inputs may be any that keep to these rules, and one draw needn't show every extreme that they name: `batch_index`: row numbers of training points, 2048 in each step; a row may repeat within a step, and rows of low-numbered devices are drawn far more often than others.
All inputs are finite; a program needn't handle non-finite values.
Results may differ from a plain program's by a relative error of at most 0.0042.
Values sent between devices are 32-bit elements; how exact they have to be, the bound alone decides.
No kernel may reach another device: no remote copies, remote signals or barrier semaphores. Data moves between devices by JAX's collectives and lax.ppermute only.
A program may use at most 128 MiB of HBM per device.

v0:
```python
import math
import jax
import jax.numpy as jnp
from jax import lax
from jax.sharding import PartitionSpec as P

SCALE = 3.0**0.5 / 1.25


def matern_tile(points_block, queries):
    cross_term = jnp.dot(
        points_block.T, queries, precision=lax.Precision.HIGHEST, preferred_element_type=jnp.float32
    )
    sq_points = jnp.sum(points_block * points_block, axis=0)
    sq_queries = jnp.sum(queries * queries, axis=0)
    dist_sq = jnp.maximum(sq_points[:, None] + sq_queries[None, :] - 2.0 * cross_term, 0.0)
    scaled = SCALE * jnp.sqrt(dist_sq)
    return ((1.0 + scaled) * jnp.exp(-scaled)).astype(jnp.bfloat16)


def kernel_times(points, coeff_half, queries):
    query_count = queries.shape[1]
    blk_width = math.gcd(query_count, 512)
    blocks = queries.reshape(queries.shape[0], query_count // blk_width, blk_width).transpose(
        1, 0, 2
    )

    def apply_block(block):
        return jnp.dot(coeff_half, matern_tile(points, block), preferred_element_type=jnp.float32)

    results = lax.map(apply_block, blocks)
    return results.transpose(1, 0, 2).reshape(coeff_half.shape[0], query_count)


def per_device(points, coeffs, velocity, targets, batch_index, test_points):
    local_count = points.shape[1]
    row_start = lax.axis_index(("rows", "cols")) * local_count

    def take_owned(array, safe_rows, weights):
        return jnp.take(array, safe_rows, axis=1) * weights[None, :]

    steps_total = batch_index.shape[0]
    coeffs_now = coeffs
    velocity_now = velocity
    for step_no in range(steps_total):
        picked = batch_index[step_no]
        offset = picked - row_start
        inside = (offset >= 0) & (offset < local_count)
        owned_safe_rows = jnp.clip(offset, 0, local_count - 1)
        safe_rows = owned_safe_rows
        weights = inside.astype(jnp.float32)
        batch_points = lax.psum(take_owned(points, safe_rows, weights), ("rows", "cols"))
        partial_sums = kernel_times(points, coeffs_now.astype(jnp.bfloat16), batch_points)
        own_terms = take_owned(coeffs_now, safe_rows, weights) * 1.0 - take_owned(
            targets, safe_rows, weights
        )
        gradient = lax.psum(partial_sums + own_terms, ("rows", "cols"))
        summed = jnp.zeros_like(coeffs_now).at[:, safe_rows].add(gradient * weights[None, :])
        velocity_now = 0.9 * velocity_now - 0.5 * summed
        coeffs_now = coeffs_now + velocity_now
    coeff_half = coeffs_now.astype(jnp.bfloat16)
    partial_test = kernel_times(
        points, coeff_half, lax.all_gather(test_points, "cols", axis=1, tiled=True)
    )
    slab_sum = lax.psum_scatter(partial_test, "cols", scatter_dimension=1, tiled=True)
    slab_sum = lax.psum(slab_sum, "rows")
    return (coeffs_now, velocity_now, slab_sum)


def solution(mesh):
    return jax.shard_map(
        per_device,
        mesh=mesh,
        in_specs=(
            P(None, ("rows", "cols")),
            P(None, ("rows", "cols")),
            P(None, ("rows", "cols")),
            P(None, ("rows", "cols")),
            P(),
            P(None, "cols"),
        ),
        out_specs=(P(None, ("rows", "cols")), P(None, ("rows", "cols")), P(None, "cols")),
        check_vma=False,
    )
```

profile of v0, /device:TPU:1, one launch (start us, length us, event | category | flops | bytes accessed | tf_op | source)
XLA Modules:
  0.0 1088.0 jit_solution(15402246799207417307)
XLA Ops:
  9.6 3.5 copy.26
  13.1 9.8 gather_fusion
  25.7 9.8 gather_fusion.3
  40.1 3.6 copy.30
  43.7 9.8 gather_fusion.2
  53.6 9.8 gather_fusion.1
  64.4 104.7 %all-reduce.6.cloned.1.call-done = f32[4,16,512]{2,1,0:T(8,128)} async-done(((f32[4,16,512]{2,1,0:T(8,128)}), f32[4,16,512]{2,1,0:T(8,128)}) %all-reduce.6.cloned.1.call-update) | async-done | bytes 131088 | tf_op jit(solution)/shard_map/psum | solution.py:52
  169.1 109.0 %while.36 = (s32[]{:T(128)}, f32[4,32,512]{2,1,0:T(8,128)S(1)}, f32[8192]{0:T(1024)S(1)}, f32[4,16,512]{2,1,0:T(8,128)}, f32[16,8192]{1,0:T(8,128)S(1)}, /*index=5*/bf16[32,8192]{1,0:T(8,128)(2,1)S(1)}, s32[]{:T(128)}) while((s32[]{:T(128)}, f32[4,32,512]{2,1,0:T(8,128)S(1)}, f32[8192]{0:T(1024)S(1)}, f32[4,16,512]{2,1,0:T(8,128)}, ...), condition=%wide.region_4.6_spmd, body=%wide.region_2.5_spmd.sunk | while | flops 1111506432 | bytes 17993824 | solution.py:31
  170.0 23.8 %multiply_convert_fusion.6 = bf16[8192,512]{0,1:T(8,128)(2,1)S(1)} fusion(f32[16,8192]{1,0:T(8,128)S(1)} %get-tuple-element.416, f32[512]{0:T(512)S(1)} %fusion.69, f32[8192]{0:T(1024)S(1)} %get-tuple-element.414, f32[4,16,512]{2,1,0:T(8,128)} %get-tuple-element.415, s32[]{:T(128)S(6)} %copy.59), kind=kOutput, calls=%fused_computation.12.clone.1 | convolution fusion | flops 843055104 | bytes 8980484 | tf_op jit(solution)/shard_map/while/body/eval_jaxpr/dot_general | solution.py:11
  197.2 23.8 %multiply_convert_fusion.6 = bf16[8192,512]{0,1:T(8,128)(2,1)S(1)} fusion(f32[16,8192]{1,0:T(8,128)S(1)} %get-tuple-element.416, f32[512]{0:T(512)S(1)} %fusion.69, f32[8192]{0:T(1024)S(1)} %get-tuple-element.414, f32[4,16,512]{2,1,0:T(8,128)} %get-tuple-element.415, s32[]{:T(128)S(6)} %copy.59), kind=kOutput, calls=%fused_computation.12.clone.1 | convolution fusion | flops 843055104 | bytes 8980484 | tf_op jit(solution)/shard_map/while/body/eval_jaxpr/dot_general | solution.py:11
  224.4 23.8 %multiply_convert_fusion.6 = bf16[8192,512]{0,1:T(8,128)(2,1)S(1)} fusion(f32[16,8192]{1,0:T(8,128)S(1)} %get-tuple-element.416, f32[512]{0:T(512)S(1)} %fusion.69, f32[8192]{0:T(1024)S(1)} %get-tuple-element.414, f32[4,16,512]{2,1,0:T(8,128)} %get-tuple-element.415, s32[]{:T(128)S(6)} %copy.59), kind=kOutput, calls=%fused_computation.12.clone.1 | convolution fusion | flops 843055104 | bytes 8980484 | tf_op jit(solution)/shard_map/while/body/eval_jaxpr/dot_general | solution.py:11
  251.6 23.8 %multiply_convert_fusion.6 = bf16[8192,512]{0,1:T(8,128)(2,1)S(1)} fusion(f32[16,8192]{1,0:T(8,128)S(1)} %get-tuple-element.416, f32[512]{0:T(512)S(1)} %fusion.69, f32[8192]{0:T(1024)S(1)} %get-tuple-element.414, f32[4,16,512]{2,1,0:T(8,128)} %get-tuple-element.415, s32[]{:T(128)S(6)} %copy.59), kind=kOutput, calls=%fused_computation.12.clone.1 | convolution fusion | flops 843055104 | bytes 8980484 | tf_op jit(solution)/shard_map/while/body/eval_jaxpr/dot_general | solution.py:11
  281.3 9.8 gather_fusion.5
  291.1 3.6 copy.25
  294.7 131.7 %all-reduce.12.cloned.1.call-done = (f32[32,2048]{0,1:T(8,128)}, f32[4,16,512]{2,1,0:T(8,128)}) async-done(((f32[32,2048]{0,1:T(8,128)}, f32[4,16,512]{2,1,0:T(8,128)}), (f32[32,2048]{0,1:T(8,128)}, f32[4,16,512]{2,1,0:T(8,128)})) %all-reduce.12.cloned.1.call-update) | async-done | bytes 393232 | tf_op jit(solution)/shard_map/psum | solution.py:57
  426.4 15.7 %scatter_custom_fusion = f32[32,8192]{0,1:T(8,128)} fusion(s32[2048]{0:T(1024)S(1)} %bitcast.194, f32[]{:T(128)} %constant.138.clone.1, f32[32,2048]{0,1:T(8,128)} %get-tuple-element.272, f32[2048]{0:T(1024)S(1)} %bitcast.188), kind=kCustom, calls=%fused_computation.46 | custom fusion | flops 131072 | bytes 1318916 | tf_op jit(solution)/shard_map/scatter-add | solution.py:58
  442.1 7.4 fusion.38
  450.4 102.8 %while.37 = (s32[]{:T(128)}, f32[4,32,512]{2,1,0:T(8,128)S(1)}, f32[8192]{0:T(1024)S(1)}, f32[4,16,512]{2,1,0:T(8,128)S(1)}, f32[16,8192]{1,0:T(8,128)S(1)}, /*index=5*/bf16[32,8192]{1,0:T(8,128)(2,1)S(1)}, s32[]{:T(128)}) while((s32[]{:T(128)}, f32[4,32,512]{2,1,0:T(8,128)S(1)}, f32[8192]{0:T(1024)S(1)}, f32[4,16,512]{2,1,0:T(8,128)S(1)}, ...), condition=%wide.region_10.13_spmd, body=%wide.region_8.12_spmd.sunk | while | flops 1111506432 | bytes 17993824 | solution.py:31
  450.4 23.0 %multiply_convert_fusion.7 = bf16[8192,512]{0,1:T(8,128)(2,1)S(1)} fusion(f32[16,8192]{1,0:T(8,128)S(1)} %get-tuple-element.437, f32[512]{0:T(512)S(1)} %fusion.75, f32[8192]{0:T(1024)S(1)} %get-tuple-element.435, f32[4,16,512]{2,1,0:T(8,128)S(1)} %get-tuple-element.436, s32[]{:T(128)S(6)} %copy.67), kind=kOutput, calls=%fused_computation.24.clone.1 | convolution fusion | flops 843055104 | bytes 8980484 | tf_op jit(solution)/shard_map/while/body/eval_jaxpr/dot_general | solution.py:11
  476.1 23.1 %multiply_convert_fusion.7 = bf16[8192,512]{0,1:T(8,128)(2,1)S(1)} fusion(f32[16,8192]{1,0:T(8,128)S(1)} %get-tuple-element.437, f32[512]{0:T(512)S(1)} %fusion.75, f32[8192]{0:T(1024)S(1)} %get-tuple-element.435, f32[4,16,512]{2,1,0:T(8,128)S(1)} %get-tuple-element.436, s32[]{:T(128)S(6)} %copy.67), kind=kOutput, calls=%fused_computation.24.clone.1 | convolution fusion | flops 843055104 | bytes 8980484 | tf_op jit(solution)/shard_map/while/body/eval_jaxpr/dot_general | solution.py:11
  501.8 23.1 %multiply_convert_fusion.7 = bf16[8192,512]{0,1:T(8,128)(2,1)S(1)} fusion(f32[16,8192]{1,0:T(8,128)S(1)} %get-tuple-element.437, f32[512]{0:T(512)S(1)} %fusion.75, f32[8192]{0:T(1024)S(1)} %get-tuple-element.435, f32[4,16,512]{2,1,0:T(8,128)S(1)} %get-tuple-element.436, s32[]{:T(128)S(6)} %copy.67), kind=kOutput, calls=%fused_computation.24.clone.1 | convolution fusion | flops 843055104 | bytes 8980484 | tf_op jit(solution)/shard_map/while/body/eval_jaxpr/dot_general | solution.py:11
  527.5 23.1 %multiply_convert_fusion.7 = bf16[8192,512]{0,1:T(8,128)(2,1)S(1)} fusion(f32[16,8192]{1,0:T(8,128)S(1)} %get-tuple-element.437, f32[512]{0:T(512)S(1)} %fusion.75, f32[8192]{0:T(1024)S(1)} %get-tuple-element.435, f32[4,16,512]{2,1,0:T(8,128)S(1)} %get-tuple-element.436, s32[]{:T(128)S(6)} %copy.67), kind=kOutput, calls=%fused_computation.24.clone.1 | convolution fusion | flops 843055104 | bytes 8980484 | tf_op jit(solution)/shard_map/while/body/eval_jaxpr/dot_general | solution.py:11
  553.5 9.8 gather_fusion.4
  566.0 10.1 all_gather.3
  576.3 138.1 %all-reduce.8.cloned.1.call-done = f32[32,2048]{0,1:T(8,128)} async-done(((f32[32,2048]{0,1:T(8,128)}), f32[32,2048]{0,1:T(8,128)}) %all-reduce.8.cloned.1.call-update) | async-done | bytes 262160 | tf_op jit(solution)/shard_map/psum | solution.py:57
  714.3 15.7 %scatter_custom_fusion.1 = f32[32,8192]{0,1:T(8,128)} fusion(s32[2048]{0:T(1024)} %bitcast.193, f32[]{:T(128)} %constant.138.clone.1, f32[32,2048]{0,1:T(8,128)} %all-reduce.8.cloned.1.call-done, f32[2048]{0:T(1024)S(1)} %bitcast.185), kind=kCustom, calls=%fused_computation.44 | custom fusion | flops 131072 | bytes 2105856 | tf_op jit(solution)/shard_map/scatter-add | solution.py:58
  730.0 10.3 fusion.37
  741.1 210.8 %while.38 = (s32[]{:T(128)}, f32[8,32,512]{2,1,0:T(8,128)}, f32[8192]{0:T(1024)S(1)}, f32[8,16,512]{2,0,1:T(8,128)S(1)}, f32[16,8192]{1,0:T(8,128)S(1)}, /*index=5*/bf16[32,8192]{1,0:T(8,128)(2,1)S(1)}, s32[]{:T(128)}) while((s32[]{:T(128)}, f32[8,32,512]{2,1,0:T(8,128)}, f32[8192]{0:T(1024)S(1)}, f32[8,16,512]{2,0,1:T(8,128)S(1)}, ...), condition=%wide.region_15.18_spmd, body=%wide.region_13.17_spmd.sunk | while | flops 1111506432 | bytes 18059356 | solution.py:31
  741.2 23.0 %multiply_convert_fusion.8 = bf16[8192,512]{0,1:T(8,128)(2,1)S(1)} fusion(f32[16,8192]{1,0:T(8,128)S(1)} %get-tuple-element.458, f32[512]{0:T(512)S(1)} %multiply_reduce_fusion.3, f32[8192]{0:T(1024)S(1)} %get-tuple-element.456, f32[1,16,512]{2,0,1:T(1,128)S(1)} %constant_dynamic-slice_fusion.2), kind=kOutput, calls=%fused_computation.36.clone.1 | convolution fusion | flops 843055104 | bytes 8980480 | tf_op jit(solution)/shard_map/while/body/eval_jaxpr/dot_general | solution.py:11
  764.2 3.2 fusion.80
  767.5 23.0 %multiply_convert_fusion.8 = bf16[8192,512]{0,1:T(8,128)(2,1)S(1)} fusion(f32[16,8192]{1,0:T(8,128)S(1)} %get-tuple-element.458, f32[512]{0:T(512)S(1)} %multiply_reduce_fusion.3, f32[8192]{0:T(1024)S(1)} %get-tuple-element.456, f32[1,16,512]{2,0,1:T(1,128)S(1)} %constant_dynamic-slice_fusion.2), kind=kOutput, calls=%fused_computation.36.clone.1 | convolution fusion | flops 843055104 | bytes 8980480 | tf_op jit(solution)/shard_map/while/body/eval_jaxpr/dot_general | solution.py:11
  790.6 3.2 fusion.80
  793.9 23.0 %multiply_convert_fusion.8 = bf16[8192,512]{0,1:T(8,128)(2,1)S(1)} fusion(f32[16,8192]{1,0:T(8,128)S(1)} %get-tuple-element.458, f32[512]{0:T(512)S(1)} %multiply_reduce_fusion.3, f32[8192]{0:T(1024)S(1)} %get-tuple-element.456, f32[1,16,512]{2,0,1:T(1,128)S(1)} %constant_dynamic-slice_fusion.2), kind=kOutput, calls=%fused_computation.36.clone.1 | convolution fusion | flops 843055104 | bytes 8980480 | tf_op jit(solution)/shard_map/while/body/eval_jaxpr/dot_general | solution.py:11
  816.9 3.2 fusion.80
  820.2 23.0 %multiply_convert_fusion.8 = bf16[8192,512]{0,1:T(8,128)(2,1)S(1)} fusion(f32[16,8192]{1,0:T(8,128)S(1)} %get-tuple-element.458, f32[512]{0:T(512)S(1)} %multiply_reduce_fusion.3, f32[8192]{0:T(1024)S(1)} %get-tuple-element.456, f32[1,16,512]{2,0,1:T(1,128)S(1)} %constant_dynamic-slice_fusion.2), kind=kOutput, calls=%fused_computation.36.clone.1 | convolution fusion | flops 843055104 | bytes 8980480 | tf_op jit(solution)/shard_map/while/body/eval_jaxpr/dot_general | solution.py:11
  843.3 3.2 fusion.80
  846.6 23.0 %multiply_convert_fusion.8 = bf16[8192,512]{0,1:T(8,128)(2,1)S(1)} fusion(f32[16,8192]{1,0:T(8,128)S(1)} %get-tuple-element.458, f32[512]{0:T(512)S(1)} %multiply_reduce_fusion.3, f32[8192]{0:T(1024)S(1)} %get-tuple-element.456, f32[1,16,512]{2,0,1:T(1,128)S(1)} %constant_dynamic-slice_fusion.2), kind=kOutput, calls=%fused_computation.36.clone.1 | convolution fusion | flops 843055104 | bytes 8980480 | tf_op jit(solution)/shard_map/while/body/eval_jaxpr/dot_general | solution.py:11
  869.6 3.2 fusion.80
  872.9 23.0 %multiply_convert_fusion.8 = bf16[8192,512]{0,1:T(8,128)(2,1)S(1)} fusion(f32[16,8192]{1,0:T(8,128)S(1)} %get-tuple-element.458, f32[512]{0:T(512)S(1)} %multiply_reduce_fusion.3, f32[8192]{0:T(1024)S(1)} %get-tuple-element.456, f32[1,16,512]{2,0,1:T(1,128)S(1)} %constant_dynamic-slice_fusion.2), kind=kOutput, calls=%fused_computation.36.clone.1 | convolution fusion | flops 843055104 | bytes 8980480 | tf_op jit(solution)/shard_map/while/body/eval_jaxpr/dot_general | solution.py:11
  896.0 3.2 fusion.80
  899.3 23.0 %multiply_convert_fusion.8 = bf16[8192,512]{0,1:T(8,128)(2,1)S(1)} fusion(f32[16,8192]{1,0:T(8,128)S(1)} %get-tuple-element.458, f32[512]{0:T(512)S(1)} %multiply_reduce_fusion.3, f32[8192]{0:T(1024)S(1)} %get-tuple-element.456, f32[1,16,512]{2,0,1:T(1,128)S(1)} %constant_dynamic-slice_fusion.2), kind=kOutput, calls=%fused_computation.36.clone.1 | convolution fusion | flops 843055104 | bytes 8980480 | tf_op jit(solution)/shard_map/while/body/eval_jaxpr/dot_general | solution.py:11
  922.3 3.2 fusion.80
  925.6 23.0 %multiply_convert_fusion.8 = bf16[8192,512]{0,1:T(8,128)(2,1)S(1)} fusion(f32[16,8192]{1,0:T(8,128)S(1)} %get-tuple-element.458, f32[512]{0:T(512)S(1)} %multiply_reduce_fusion.3, f32[8192]{0:T(1024)S(1)} %get-tuple-element.456, f32[1,16,512]{2,0,1:T(1,128)S(1)} %constant_dynamic-slice_fusion.2), kind=kOutput, calls=%fused_computation.36.clone.1 | convolution fusion | flops 843055104 | bytes 8980480 | tf_op jit(solution)/shard_map/while/body/eval_jaxpr/dot_general | solution.py:11
  948.6 3.2 fusion.80
  953.8 21.0 %reduce-scatter.2.cloned.1.call-done = f32[32,1024]{1,0:T(8,128)} async-done(((f32[32,4096]{1,0:T(8,128)}), f32[32,1024]{1,0:T(8,128)}) %reduce-scatter.2.cloned.1.call-update) | async-done | bytes 131088 | tf_op jit(solution)/shard_map/reduce_scatter | solution.py:65
  974.8 3.6 copy.40
  978.4 3.6 copy.41
  982.0 97.5 %all-reduce.10.cloned.1.call-done = f32[32,1024]{1,0:T(8,128)} async-done(((f32[32,1024]{1,0:T(8,128)}), f32[32,1024]{1,0:T(8,128)}) %all-reduce.10.cloned.1.call-update) | async-done | bytes 131088 | tf_op jit(solution)/shard_map/psum | solution.py:66
  (87 shorter events, 46.6 us)
Async XLA Ops:
  7.2 30.1 %copy-start.1 = (f32[16,8192]{1,0:T(8,128)S(1)}, f32[16,8192]{1,0:T(8,128)}, u32[]{:S(2)}) copy-start(f32[16,8192]{1,0:T(8,128)} %param.16) | copy-start | bytes 1572868
  7.2 30.2 %copy-start = (f32[32,8192]{1,0:T(8,128)S(1)}, f32[32,8192]{1,0:T(8,128)}, u32[]{:S(2)}) copy-start(f32[32,8192]{1,0:T(8,128)} %param.17) | copy-start | bytes 3145732
  7.2 161.9 %all-reduce.6.cloned.1.call-start = ((), (), s32[]{:S(2)}) async-start(), calls=%async_computation.1 | async-start | bytes 262144 | tf_op jit(solution)/shard_map/psum | solution.py:52
  8.1 29.2 %copy-start.5 = (f32[1,2048]{1,0:T(1,128)}, f32[1,2048]{1,0:T(1,128)S(1)}, u32[]{:S(2)}) copy-start(f32[1,2048]{1,0:T(1,128)S(1)} %get-tuple-element.283) | copy-start | bytes 24580
  25.6 400.7 %all-reduce.12.cloned.1.call-start = ((), (), s32[]{:S(2)}) async-start(), calls=%async_computation.5 | async-start | bytes 2359296 | tf_op jit(solution)/shard_map/psum | solution.py:57
  25.7 27.9 %copy-start.8 = (pred[2048]{0:T(1024)(128)(4,1)}, pred[2048]{0:T(1024)(128)(4,1)S(1)}, u32[]{:S(2)}) copy-start(pred[2048]{0:T(1024)(128)(4,1)S(1)} %compare_and_fusion) | copy-start | bytes 6148
  169.1 109.3 %copy-start.3 = (f32[2048,32]{1,0:T(8,128)S(1)}, f32[2048,32]{1,0:T(8,128)}, u32[]{:S(2)}) copy-start(f32[2048,32]{1,0:T(8,128)} %gather_fusion.2) | copy-start | bytes 786436
  281.0 433.3 %all-reduce.8.cloned.1.call-start = ((), (), s32[]{:S(2)}) async-start(), calls=%async_computation.2 | async-start | bytes 2097152 | tf_op jit(solution)/shard_map/psum | solution.py:57
  442.1 8.3 copy-start.4
  450.4 113.0 %copy-start.2 = (f32[2048,32]{1,0:T(8,128)S(1)}, f32[2048,32]{1,0:T(8,128)}, u32[]{:S(2)}) copy-start(f32[2048,32]{1,0:T(8,128)} %gather_fusion.5) | copy-start | bytes 786436
  450.4 113.0 %copy-start.6 = (f32[1,2048]{1,0:T(1,128)S(1)}, f32[1,2048]{1,0:T(1,128)}, u32[]{:S(2)}) copy-start(f32[1,2048]{1,0:T(1,128)} %copy-done.5) | copy-start | bytes 24580
  450.4 113.0 %copy-start.9 = (pred[2048]{0:T(1024)(128)(4,1)S(1)}, pred[2048]{0:T(1024)(128)(4,1)}, u32[]{:S(2)}) copy-start(pred[2048]{0:T(1024)(128)(4,1)} %copy-done.8) | copy-start | bytes 6148
  553.2 12.9 %copy-start.7 = (f32[16,1024]{1,0:T(8,128)S(1)}, f32[16,1024]{1,0:T(8,128)}, u32[]{:S(2)}) copy-start(f32[16,1024]{1,0:T(8,128)} %param.21) | copy-start | bytes 196612
  566.0 408.8 %reduce-scatter.2.cloned.1.call-start = ((), (), s32[]{:S(2)}) async-start(), calls=%async_computation.3 | async-start | bytes 655360 | tf_op jit(solution)/shard_map/reduce_scatter | solution.py:65
  953.8 125.7 %all-reduce.10.cloned.1.call-start = ((), (), s32[]{:S(2)}) async-start(), calls=%async_computation.4 | async-start | bytes 262144 | tf_op jit(solution)/shard_map/psum | solution.py:66
Sparse Core Ops, SparseCore 0:
  25.7 143.2 all-reduce.5
  281.2 145.1 all-reduce.11
  566.1 148.1 all-reduce.7
  953.9 20.8 reduce-scatter.1
  978.2 101.2 all-reduce.9
where the time goes:
time: 1100 us; the launch traced here: 1090 us
  waiting for transfers between devices  493 us (45%)
  matrix products  419 us (38%)
  local copies, waits for them, and re-layouts  87.6 us (8%)
  other arithmetic  63.8 us (6%)
  between operations  14.4 us (1%)
    dot_general x16, matrix products, matern_tile(): jnp.dot(points_block.T, queries, precision=lax.Precision.HIGHEST, preferr...  372 us
    psum x2, waiting for transfers between devices, per_device(): gradient = lax.psum(partial_sums + own_terms, ('rows', 'cols'))  270 us
    psum x1, waiting for transfers between devices, per_device(): lax.psum(take_owned(points, safe_rows, weights), ('rows', 'cols'))  105 us
    psum x1, waiting for transfers between devices, per_device(): slab_sum = lax.psum(slab_sum, 'rows')  97.5 us
    gather x6, local copies, waits for them, and re-layouts, take_owned(): return jnp.take(array, safe_rows, axis=1) * weights[None, :]  58.9 us
    dot_general x16, matrix products, apply_block(): jnp.dot(coeff_half, matern_tile(points, block), preferred_element_type=jn...  46.8 us
    scatter-add x2, other arithmetic, per_device(): jnp.zeros_like(coeffs_now).at[:, safe_rows].add(gradient * weights[None, :])  31.4 us
    unnamed x28, local copies, waits for them, and re-layouts  22.4 us
  transfers between devices with their start and end apart: 5, of which 5 were waited for; matrix products, arithmetic and copies ran while one was open for 5% of the time, Pallas kernels for 0%

commit v1 on v0

--- a/solution.py
+++ b/solution.py
@@ -63,7 +63,11 @@
         points, coeff_half, lax.all_gather(test_points, "cols", axis=1, tiled=True)
     )
     slab_sum = lax.psum_scatter(partial_test, "cols", scatter_dimension=1, tiled=True)
-    slab_sum = lax.psum(slab_sum, "rows")
+    slab_sum = slab_sum
+    for hop in (1, 2, 4, 8, 16):
+        slab_sum = slab_sum + lax.ppermute(
+            slab_sum, "rows", [(dev, dev ^ hop) for dev in range(32)]
+        )
     return (coeffs_now, velocity_now, slab_sum)
 
 

time: 1100 us -> 1020 us (0.927)
  waiting for transfers between devices: 493 us -> 405 us
    psum x1 -> x0, waiting for transfers between devices: 97.5 us -> none  [per_device(): slab_sum = lax.psum(slab_sum, 'rows')]
    unnamed x28 -> x27, local copies, waits for them, and re-layouts: 22.4 us -> 20.8 us
  transfers between devices with their start and end apart: 5 -> 9, of which waited for: 5 -> 8; matrix products, arithmetic and copies ran while one was open for 5% -> 6% of each run, Pallas kernels for 0% -> 0%
where the time goes in v1:
time: 1020 us; the launch traced here: 1010 us
  matrix products  419 us (41%)
  waiting for transfers between devices  405 us (40%)
  local copies, waits for them, and re-layouts  86.1 us (8%)
  other arithmetic  65.5 us (6%)
  between operations  14.4 us (1%)
  starting transfers between devices  11.2 us (1%)
    dot_general x16, matrix products, matern_tile(): jnp.dot(points_block.T, queries, precision=lax.Precision.HIGHEST, preferr...  372 us
    psum x2, waiting for transfers between devices, per_device(): gradient = lax.psum(partial_sums + own_terms, ('rows', 'cols'))  270 us
    psum x1, waiting for transfers between devices, per_device(): lax.psum(take_owned(points, safe_rows, weights), ('rows', 'cols'))  105 us
    gather x6, local copies, waits for them, and re-layouts, take_owned(): return jnp.take(array, safe_rows, axis=1) * weights[None, :]  58.9 us
    dot_general x16, matrix products, apply_block(): jnp.dot(coeff_half, matern_tile(points, block), preferred_element_type=jn...  46.8 us
    scatter-add x2, other arithmetic, per_device(): jnp.zeros_like(coeffs_now).at[:, safe_rows].add(gradient * weights[None, :])  31.4 us
    reduce_scatter x1, waiting for transfers between devices, per_device(): lax.psum_scatter(partial_test, 'cols', scatter_dimension=1, tiled=True)  21 us
    unnamed x27, local copies, waits for them, and re-layouts  20.8 us
  transfers between devices with their start and end apart: 9, of which 8 were waited for; matrix products, arithmetic and copies ran while one was open for 6% of the time, Pallas kernels for 0%

profile of v1, /device:TPU:1, one launch (start us, length us, event | category | flops | bytes accessed | tf_op | source)
XLA Modules:
  0.0 1011.1 jit_solution(12448964507558421555)
XLA Ops:
  9.6 3.5 copy.26
  13.1 9.8 gather_fusion
  25.7 9.8 gather_fusion.3
  40.1 3.6 copy.30
  43.8 9.8 gather_fusion.2
  53.6 9.8 gather_fusion.1
  64.4 104.7 %all-reduce.5.cloned.1.call-done = f32[4,16,512]{2,1,0:T(8,128)} async-done(((f32[4,16,512]{2,1,0:T(8,128)}), f32[4,16,512]{2,1,0:T(8,128)}) %all-reduce.5.cloned.1.call-update) | async-done | bytes 131088 | tf_op jit(solution)/shard_map/psum | solution.py:52
  169.1 109.0 %while.36 = (s32[]{:T(128)}, f32[4,32,512]{2,1,0:T(8,128)S(1)}, f32[8192]{0:T(1024)S(1)}, f32[4,16,512]{2,1,0:T(8,128)}, f32[16,8192]{1,0:T(8,128)S(1)}, /*index=5*/bf16[32,8192]{1,0:T(8,128)(2,1)S(1)}, s32[]{:T(128)}) while((s32[]{:T(128)}, f32[4,32,512]{2,1,0:T(8,128)S(1)}, f32[8192]{0:T(1024)S(1)}, f32[4,16,512]{2,1,0:T(8,128)}, ...), condition=%wide.region_4.6_spmd, body=%wide.region_2.5_spmd.sunk | while | flops 1111506432 | bytes 17993824 | solution.py:31
  170.0 23.8 %multiply_convert_fusion.6 = bf16[8192,512]{0,1:T(8,128)(2,1)S(1)} fusion(f32[16,8192]{1,0:T(8,128)S(1)} %get-tuple-element.416, f32[512]{0:T(512)S(1)} %fusion.69, f32[8192]{0:T(1024)S(1)} %get-tuple-element.414, f32[4,16,512]{2,1,0:T(8,128)} %get-tuple-element.415, s32[]{:T(128)S(6)} %copy.59), kind=kOutput, calls=%fused_computation.12.clone.1 | convolution fusion | flops 843055104 | bytes 8980484 | tf_op jit(solution)/shard_map/while/body/eval_jaxpr/dot_general | solution.py:11
  197.2 23.8 %multiply_convert_fusion.6 = bf16[8192,512]{0,1:T(8,128)(2,1)S(1)} fusion(f32[16,8192]{1,0:T(8,128)S(1)} %get-tuple-element.416, f32[512]{0:T(512)S(1)} %fusion.69, f32[8192]{0:T(1024)S(1)} %get-tuple-element.414, f32[4,16,512]{2,1,0:T(8,128)} %get-tuple-element.415, s32[]{:T(128)S(6)} %copy.59), kind=kOutput, calls=%fused_computation.12.clone.1 | convolution fusion | flops 843055104 | bytes 8980484 | tf_op jit(solution)/shard_map/while/body/eval_jaxpr/dot_general | solution.py:11
  224.4 23.8 %multiply_convert_fusion.6 = bf16[8192,512]{0,1:T(8,128)(2,1)S(1)} fusion(f32[16,8192]{1,0:T(8,128)S(1)} %get-tuple-element.416, f32[512]{0:T(512)S(1)} %fusion.69, f32[8192]{0:T(1024)S(1)} %get-tuple-element.414, f32[4,16,512]{2,1,0:T(8,128)} %get-tuple-element.415, s32[]{:T(128)S(6)} %copy.59), kind=kOutput, calls=%fused_computation.12.clone.1 | convolution fusion | flops 843055104 | bytes 8980484 | tf_op jit(solution)/shard_map/while/body/eval_jaxpr/dot_general | solution.py:11
  251.7 23.8 %multiply_convert_fusion.6 = bf16[8192,512]{0,1:T(8,128)(2,1)S(1)} fusion(f32[16,8192]{1,0:T(8,128)S(1)} %get-tuple-element.416, f32[512]{0:T(512)S(1)} %fusion.69, f32[8192]{0:T(1024)S(1)} %get-tuple-element.414, f32[4,16,512]{2,1,0:T(8,128)} %get-tuple-element.415, s32[]{:T(128)S(6)} %copy.59), kind=kOutput, calls=%fused_computation.12.clone.1 | convolution fusion | flops 843055104 | bytes 8980484 | tf_op jit(solution)/shard_map/while/body/eval_jaxpr/dot_general | solution.py:11
  281.3 9.8 gather_fusion.5
  291.1 3.6 copy.25
  294.7 131.7 %all-reduce.9.cloned.1.call-done = (f32[32,2048]{0,1:T(8,128)}, f32[4,16,512]{2,1,0:T(8,128)}) async-done(((f32[32,2048]{0,1:T(8,128)}, f32[4,16,512]{2,1,0:T(8,128)}), (f32[32,2048]{0,1:T(8,128)}, f32[4,16,512]{2,1,0:T(8,128)})) %all-reduce.9.cloned.1.call-update) | async-done | bytes 393232 | tf_op jit(solution)/shard_map/psum | solution.py:57
  426.4 15.7 %scatter_custom_fusion = f32[32,8192]{0,1:T(8,128)} fusion(s32[2048]{0:T(1024)S(1)} %bitcast.194, f32[]{:T(128)} %constant.138.clone.1, f32[32,2048]{0,1:T(8,128)} %get-tuple-element.272, f32[2048]{0:T(1024)S(1)} %bitcast.188), kind=kCustom, calls=%fused_computation.46 | custom fusion | flops 131072 | bytes 1318916 | tf_op jit(solution)/shard_map/scatter-add | solution.py:58
  442.1 7.4 fusion.38
  450.4 102.8 %while.37 = (s32[]{:T(128)}, f32[4,32,512]{2,1,0:T(8,128)S(1)}, f32[8192]{0:T(1024)S(1)}, f32[4,16,512]{2,1,0:T(8,128)S(1)}, f32[16,8192]{1,0:T(8,128)S(1)}, /*index=5*/bf16[32,8192]{1,0:T(8,128)(2,1)S(1)}, s32[]{:T(128)}) while((s32[]{:T(128)}, f32[4,32,512]{2,1,0:T(8,128)S(1)}, f32[8192]{0:T(1024)S(1)}, f32[4,16,512]{2,1,0:T(8,128)S(1)}, ...), condition=%wide.region_10.13_spmd, body=%wide.region_8.12_spmd.sunk | while | flops 1111506432 | bytes 17993824 | solution.py:31
  450.5 23.1 %multiply_convert_fusion.7 = bf16[8192,512]{0,1:T(8,128)(2,1)S(1)} fusion(f32[16,8192]{1,0:T(8,128)S(1)} %get-tuple-element.437, f32[512]{0:T(512)S(1)} %fusion.75, f32[8192]{0:T(1024)S(1)} %get-tuple-element.435, f32[4,16,512]{2,1,0:T(8,128)S(1)} %get-tuple-element.436, s32[]{:T(128)S(6)} %copy.67), kind=kOutput, calls=%fused_computation.24.clone.1 | convolution fusion | flops 843055104 | bytes 8980484 | tf_op jit(solution)/shard_map/while/body/eval_jaxpr/dot_general | solution.py:11
  476.2 23.1 %multiply_convert_fusion.7 = bf16[8192,512]{0,1:T(8,128)(2,1)S(1)} fusion(f32[16,8192]{1,0:T(8,128)S(1)} %get-tuple-element.437, f32[512]{0:T(512)S(1)} %fusion.75, f32[8192]{0:T(1024)S(1)} %get-tuple-element.435, f32[4,16,512]{2,1,0:T(8,128)S(1)} %get-tuple-element.436, s32[]{:T(128)S(6)} %copy.67), kind=kOutput, calls=%fused_computation.24.clone.1 | convolution fusion | flops 843055104 | bytes 8980484 | tf_op jit(solution)/shard_map/while/body/eval_jaxpr/dot_general | solution.py:11
  501.9 23.1 %multiply_convert_fusion.7 = bf16[8192,512]{0,1:T(8,128)(2,1)S(1)} fusion(f32[16,8192]{1,0:T(8,128)S(1)} %get-tuple-element.437, f32[512]{0:T(512)S(1)} %fusion.75, f32[8192]{0:T(1024)S(1)} %get-tuple-element.435, f32[4,16,512]{2,1,0:T(8,128)S(1)} %get-tuple-element.436, s32[]{:T(128)S(6)} %copy.67), kind=kOutput, calls=%fused_computation.24.clone.1 | convolution fusion | flops 843055104 | bytes 8980484 | tf_op jit(solution)/shard_map/while/body/eval_jaxpr/dot_general | solution.py:11
  527.6 23.1 %multiply_convert_fusion.7 = bf16[8192,512]{0,1:T(8,128)(2,1)S(1)} fusion(f32[16,8192]{1,0:T(8,128)S(1)} %get-tuple-element.437, f32[512]{0:T(512)S(1)} %fusion.75, f32[8192]{0:T(1024)S(1)} %get-tuple-element.435, f32[4,16,512]{2,1,0:T(8,128)S(1)} %get-tuple-element.436, s32[]{:T(128)S(6)} %copy.67), kind=kOutput, calls=%fused_computation.24.clone.1 | convolution fusion | flops 843055104 | bytes 8980484 | tf_op jit(solution)/shard_map/while/body/eval_jaxpr/dot_general | solution.py:11
  553.6 9.8 gather_fusion.4
  566.1 10.1 all_gather.3
  576.3 138.1 %all-reduce.7.cloned.1.call-done = f32[32,2048]{0,1:T(8,128)} async-done(((f32[32,2048]{0,1:T(8,128)}), f32[32,2048]{0,1:T(8,128)}) %all-reduce.7.cloned.1.call-update) | async-done | bytes 262160 | tf_op jit(solution)/shard_map/psum | solution.py:57
  714.4 15.7 %scatter_custom_fusion.1 = f32[32,8192]{0,1:T(8,128)} fusion(s32[2048]{0:T(1024)} %bitcast.193, f32[]{:T(128)} %constant.138.clone.1, f32[32,2048]{0,1:T(8,128)} %all-reduce.7.cloned.1.call-done, f32[2048]{0:T(1024)S(1)} %bitcast.185), kind=kCustom, calls=%fused_computation.44 | custom fusion | flops 131072 | bytes 2105856 | tf_op jit(solution)/shard_map/scatter-add | solution.py:58
  730.0 10.3 %fusion.37 = (bf16[32,8192]{0,1:T(8,128)(2,1)S(1)}, f32[32,8192]{0,1:T(8,128)}, f32[32,8192]{0,1:T(8,128)}) fusion(f32[32,8192]{0,1:T(8,128)} %get-tuple-element.278, f32[32,8192]{0,1:T(8,128)} %scatter_custom_fusion.1, f32[32,8192]{0,1:T(8,128)} %scatter_custom_fusion, f32[32,8192]{0,1:T(8,128)} %copy.25), kind=kLoop, calls=%fused_computation.80 | loop fusion | flops 2097152 | bytes 6815744 | tf_op jit(solution)/shard_map/convert_element_type | solution.py:61
  741.2 210.8 %while.38 = (s32[]{:T(128)}, f32[8,32,512]{2,1,0:T(8,128)}, f32[8192]{0:T(1024)S(1)}, f32[8,16,512]{2,0,1:T(8,128)S(1)}, f32[16,8192]{1,0:T(8,128)S(1)}, /*index=5*/bf16[32,8192]{1,0:T(8,128)(2,1)S(1)}, s32[]{:T(128)}) while((s32[]{:T(128)}, f32[8,32,512]{2,1,0:T(8,128)}, f32[8192]{0:T(1024)S(1)}, f32[8,16,512]{2,0,1:T(8,128)S(1)}, ...), condition=%wide.region_15.18_spmd, body=%wide.region_13.17_spmd.sunk | while | flops 1111506432 | bytes 18059356 | solution.py:31
  741.3 23.0 %multiply_convert_fusion.8 = bf16[8192,512]{0,1:T(8,128)(2,1)S(1)} fusion(f32[16,8192]{1,0:T(8,128)S(1)} %get-tuple-element.458, f32[512]{0:T(512)S(1)} %multiply_reduce_fusion.3, f32[8192]{0:T(1024)S(1)} %get-tuple-element.456, f32[1,16,512]{2,0,1:T(1,128)S(1)} %constant_dynamic-slice_fusion.2), kind=kOutput, calls=%fused_computation.36.clone.1 | convolution fusion | flops 843055104 | bytes 8980480 | tf_op jit(solution)/shard_map/while/body/eval_jaxpr/dot_general | solution.py:11
  764.3 3.2 fusion.80
  767.6 23.0 %multiply_convert_fusion.8 = bf16[8192,512]{0,1:T(8,128)(2,1)S(1)} fusion(f32[16,8192]{1,0:T(8,128)S(1)} %get-tuple-element.458, f32[512]{0:T(512)S(1)} %multiply_reduce_fusion.3, f32[8192]{0:T(1024)S(1)} %get-tuple-element.456, f32[1,16,512]{2,0,1:T(1,128)S(1)} %constant_dynamic-slice_fusion.2), kind=kOutput, calls=%fused_computation.36.clone.1 | convolution fusion | flops 843055104 | bytes 8980480 | tf_op jit(solution)/shard_map/while/body/eval_jaxpr/dot_general | solution.py:11
  790.6 3.2 fusion.80
  793.9 23.0 %multiply_convert_fusion.8 = bf16[8192,512]{0,1:T(8,128)(2,1)S(1)} fusion(f32[16,8192]{1,0:T(8,128)S(1)} %get-tuple-element.458, f32[512]{0:T(512)S(1)} %multiply_reduce_fusion.3, f32[8192]{0:T(1024)S(1)} %get-tuple-element.456, f32[1,16,512]{2,0,1:T(1,128)S(1)} %constant_dynamic-slice_fusion.2), kind=kOutput, calls=%fused_computation.36.clone.1 | convolution fusion | flops 843055104 | bytes 8980480 | tf_op jit(solution)/shard_map/while/body/eval_jaxpr/dot_general | solution.py:11
  817.0 3.2 fusion.80
  820.3 23.0 %multiply_convert_fusion.8 = bf16[8192,512]{0,1:T(8,128)(2,1)S(1)} fusion(f32[16,8192]{1,0:T(8,128)S(1)} %get-tuple-element.458, f32[512]{0:T(512)S(1)} %multiply_reduce_fusion.3, f32[8192]{0:T(1024)S(1)} %get-tuple-element.456, f32[1,16,512]{2,0,1:T(1,128)S(1)} %constant_dynamic-slice_fusion.2), kind=kOutput, calls=%fused_computation.36.clone.1 | convolution fusion | flops 843055104 | bytes 8980480 | tf_op jit(solution)/shard_map/while/body/eval_jaxpr/dot_general | solution.py:11
  843.3 3.2 fusion.80
  846.6 23.0 %multiply_convert_fusion.8 = bf16[8192,512]{0,1:T(8,128)(2,1)S(1)} fusion(f32[16,8192]{1,0:T(8,128)S(1)} %get-tuple-element.458, f32[512]{0:T(512)S(1)} %multiply_reduce_fusion.3, f32[8192]{0:T(1024)S(1)} %get-tuple-element.456, f32[1,16,512]{2,0,1:T(1,128)S(1)} %constant_dynamic-slice_fusion.2), kind=kOutput, calls=%fused_computation.36.clone.1 | convolution fusion | flops 843055104 | bytes 8980480 | tf_op jit(solution)/shard_map/while/body/eval_jaxpr/dot_general | solution.py:11
  869.7 3.2 fusion.80
  873.0 23.0 %multiply_convert_fusion.8 = bf16[8192,512]{0,1:T(8,128)(2,1)S(1)} fusion(f32[16,8192]{1,0:T(8,128)S(1)} %get-tuple-element.458, f32[512]{0:T(512)S(1)} %multiply_reduce_fusion.3, f32[8192]{0:T(1024)S(1)} %get-tuple-element.456, f32[1,16,512]{2,0,1:T(1,128)S(1)} %constant_dynamic-slice_fusion.2), kind=kOutput, calls=%fused_computation.36.clone.1 | convolution fusion | flops 843055104 | bytes 8980480 | tf_op jit(solution)/shard_map/while/body/eval_jaxpr/dot_general | solution.py:11
  896.0 3.2 fusion.80
  899.3 23.0 %multiply_convert_fusion.8 = bf16[8192,512]{0,1:T(8,128)(2,1)S(1)} fusion(f32[16,8192]{1,0:T(8,128)S(1)} %get-tuple-element.458, f32[512]{0:T(512)S(1)} %multiply_reduce_fusion.3, f32[8192]{0:T(1024)S(1)} %get-tuple-element.456, f32[1,16,512]{2,0,1:T(1,128)S(1)} %constant_dynamic-slice_fusion.2), kind=kOutput, calls=%fused_computation.36.clone.1 | convolution fusion | flops 843055104 | bytes 8980480 | tf_op jit(solution)/shard_map/while/body/eval_jaxpr/dot_general | solution.py:11
  922.3 3.2 fusion.80
  925.6 23.0 %multiply_convert_fusion.8 = bf16[8192,512]{0,1:T(8,128)(2,1)S(1)} fusion(f32[16,8192]{1,0:T(8,128)S(1)} %get-tuple-element.458, f32[512]{0:T(512)S(1)} %multiply_reduce_fusion.3, f32[8192]{0:T(1024)S(1)} %get-tuple-element.456, f32[1,16,512]{2,0,1:T(1,128)S(1)} %constant_dynamic-slice_fusion.2), kind=kOutput, calls=%fused_computation.36.clone.1 | convolution fusion | flops 843055104 | bytes 8980480 | tf_op jit(solution)/shard_map/while/body/eval_jaxpr/dot_general | solution.py:11
  948.7 3.2 fusion.80
  953.8 21.0 %reduce-scatter.2.cloned.1.call-done = f32[32,1024]{1,0:T(8,128)} async-done(((f32[32,4096]{1,0:T(8,128)}), f32[32,1024]{1,0:T(8,128)}) %reduce-scatter.2.cloned.1.call-update) | async-done | bytes 131088 | tf_op jit(solution)/shard_map/reduce_scatter | solution.py:65
  980.7 3.4 collective-permute-done.1
  996.3 3.6 copy.40
  999.9 3.6 copy.41
  (98 shorter events, 63.7 us)
Async XLA Ops:
  7.2 30.1 %copy-start.1 = (f32[16,8192]{1,0:T(8,128)S(1)}, f32[16,8192]{1,0:T(8,128)}, u32[]{:S(2)}) copy-start(f32[16,8192]{1,0:T(8,128)} %param.16) | copy-start | bytes 1572868
  7.2 30.2 %copy-start = (f32[32,8192]{1,0:T(8,128)S(1)}, f32[32,8192]{1,0:T(8,128)}, u32[]{:S(2)}) copy-start(f32[32,8192]{1,0:T(8,128)} %param.17) | copy-start | bytes 3145732
  7.2 161.9 %all-reduce.5.cloned.1.call-start = ((), (), s32[]{:S(2)}) async-start(), calls=%async_computation.1 | async-start | bytes 262144 | tf_op jit(solution)/shard_map/psum | solution.py:52
  8.1 29.2 %copy-start.5 = (f32[1,2048]{1,0:T(1,128)}, f32[1,2048]{1,0:T(1,128)S(1)}, u32[]{:S(2)}) copy-start(f32[1,2048]{1,0:T(1,128)S(1)} %get-tuple-element.283) | copy-start | bytes 24580
  25.6 400.8 %all-reduce.9.cloned.1.call-start = ((), (), s32[]{:S(2)}) async-start(), calls=%async_computation.4 | async-start | bytes 2359296 | tf_op jit(solution)/shard_map/psum | solution.py:57
  25.7 27.9 %copy-start.8 = (pred[2048]{0:T(1024)(128)(4,1)}, pred[2048]{0:T(1024)(128)(4,1)S(1)}, u32[]{:S(2)}) copy-start(pred[2048]{0:T(1024)(128)(4,1)S(1)} %compare_and_fusion) | copy-start | bytes 6148
  169.1 109.3 %copy-start.3 = (f32[2048,32]{1,0:T(8,128)S(1)}, f32[2048,32]{1,0:T(8,128)}, u32[]{:S(2)}) copy-start(f32[2048,32]{1,0:T(8,128)} %gather_fusion.2) | copy-start | bytes 786436
  281.1 433.3 %all-reduce.7.cloned.1.call-start = ((), (), s32[]{:S(2)}) async-start(), calls=%async_computation.2 | async-start | bytes 2097152 | tf_op jit(solution)/shard_map/psum | solution.py:57
  442.1 8.3 copy-start.4
  450.4 113.0 %copy-start.2 = (f32[2048,32]{1,0:T(8,128)S(1)}, f32[2048,32]{1,0:T(8,128)}, u32[]{:S(2)}) copy-start(f32[2048,32]{1,0:T(8,128)} %gather_fusion.5) | copy-start | bytes 786436
  450.4 113.0 %copy-start.6 = (f32[1,2048]{1,0:T(1,128)S(1)}, f32[1,2048]{1,0:T(1,128)}, u32[]{:S(2)}) copy-start(f32[1,2048]{1,0:T(1,128)} %copy-done.5) | copy-start | bytes 24580
  450.4 113.0 %copy-start.9 = (pred[2048]{0:T(1024)(128)(4,1)S(1)}, pred[2048]{0:T(1024)(128)(4,1)}, u32[]{:S(2)}) copy-start(pred[2048]{0:T(1024)(128)(4,1)} %copy-done.8) | copy-start | bytes 6148
  553.2 12.9 %copy-start.7 = (f32[16,1024]{1,0:T(8,128)S(1)}, f32[16,1024]{1,0:T(8,128)}, u32[]{:S(2)}) copy-start(f32[16,1024]{1,0:T(8,128)} %param.21) | copy-start | bytes 196612
  566.0 408.8 %reduce-scatter.2.cloned.1.call-start = ((), (), s32[]{:S(2)}) async-start(), calls=%async_computation.3 | async-start | bytes 655360 | tf_op jit(solution)/shard_map/reduce_scatter | solution.py:65
  974.8 3.5 collective-permute-start
  979.3 4.8 collective-permute-start.1
  984.1 5.4 collective-permute-start.2
  989.5 3.9 collective-permute-start.3
  993.4 10.0 collective-permute-start.4
Sparse Core Ops, SparseCore 0:
  25.8 143.2 all-reduce.4
  281.2 145.1 all-reduce.8
  566.2 148.1 all-reduce.6
  954.0 20.8 reduce-scatter.1
